TPU v7x, 512 devices: a whole 4x8x8 slice. The times are simulated.
512 devices in a mesh: dp: 16 (over y_hi, z), ctx: 32 (over y_lo, x, core).
Axes of the slice: x: 4, y: 8 (y_hi: 2, y_lo: 4; y = y_hi * 4 + y_lo), z: 8, core: 2. Of those that a mesh axis runs over, the one named last changes fastest.
Arguments:
- queries: bfloat16 [16, 4096, 4096], P('dp', 'ctx'), may hold values from -6 to 6
- keys: bfloat16 [16, 4096, 512], P('dp', 'ctx'), may hold values from -6 to 6
- values: bfloat16 [16, 4096, 512], P('dp', 'ctx'), may hold values from -6 to 6
- grad_out: bfloat16 [16, 4096, 4096], P('dp', 'ctx'), may hold values from -6 to 6
- doc_lengths: int32 [16, 8], P('dp'), may hold values from 1 to 2048, 4096 in all within a row
- block_of_slot: int32 [64], replicated, may hold values from 0 to 63, as said below
- partners: int32 [3, 32], replicated, may hold values from 0 to 31, as said below
Outputs:
- attended: bfloat16 [16, 4096, 4096], P('dp', 'ctx')
- grad_queries: bfloat16 [16, 4096, 4096], P('dp', 'ctx')
- grad_keys: bfloat16 [16, 4096, 512], P('dp', 'ctx')
- grad_values: bfloat16 [16, 4096, 512], P('dp', 'ctx')
Inputs may be any that keep to these rules, and one draw needn't show every extreme that they name: `block_of_slot`: slots 2k and 2k + 1 are the rows of ctx rank k and hold blocks c and 63 - c; every block appears once. `partners`: in row r every rank i has partner i XOR m_r, where m_r is a power of two, the same for all ranks of the row, and different between rows.
All inputs are finite; a program needn't handle non-finite values.
Results may differ from a plain program's by a relative error of at most 0.034.
Values may be sent and summed in bfloat16 or wider, within the bound.
No kernel may reach another device: no remote copies, remote signals or barrier semaphores. Data moves between devices by JAX's collectives and lax.ppermute only.
A program may use at most 64 MiB of HBM per device.

v0:
```python
import functools
import itertools

import jax
import jax.numpy as jnp
from jax import lax
from jax.experimental import pallas as pl
from jax.experimental.pallas import tpu as pltpu
from jax.sharding import PartitionSpec as P

HQ = 32
KVH = 4
HD = 128
GROUP = HQ // KVH
FACTOR = HD ** (-0.5)
LOG2E = 1.4426950408889634
BF16 = jnp.bfloat16
F32 = jnp.float32


def swapped(value, axis, mask):
    pairs = [(source, source ^ mask) for source in range(lax.axis_size(axis))]
    return lax.ppermute(value, axis, pairs)


def documents(place, lengths_ref):
    start = jnp.int32(0)
    doc = jnp.zeros_like(place)
    for index in range(lengths_ref.shape[1] - 1):
        start = start + lengths_ref[0, index]
        doc = doc + (place >= start).astype(jnp.int32)
    return doc


def dot(a, b):
    return jnp.dot(a, b, preferred_element_type=F32)


def dot_nt(a, b):
    return lax.dot_general(a, b, (((1,), (1,)), ((), ())), preferred_element_type=F32)


def block_places(slots_ref, rank, half):
    first, second = slots_ref[2 * rank], slots_ref[2 * rank + 1]
    low_row = pl.multiple_of(jnp.where(first < second, 0, half), half)
    high_row = pl.multiple_of(half - low_row, half)
    low, high = jnp.minimum(first, second), jnp.maximum(first, second)
    return (low * half, high * half), (pl.ds(low_row, half), pl.ds(high_row, half))


def mask_scores(theirs, lengths_ref, bias_refs, valid_refs):
    docs = lengths_ref.shape[1]
    lanes = valid_refs[0].shape[1]
    half = theirs[0][1][0].size
    lane = lax.broadcasted_iota(jnp.int32, (1, lanes), 1) % half
    row = lax.broadcasted_iota(jnp.int32, (half, 1), 0)
    for side in range(2):
        q_place = lane + theirs[0][0][side]
        q_doc = documents(q_place, lengths_ref)
        valid_refs[side][...] = (q_doc < docs - 1).astype(F32)
        for level in range(side + 1):
            for index, (starts, _) in enumerate(theirs):
                k_place = row + starts[level]
                k_doc = documents(k_place, lengths_ref)
                allowed = (k_place <= q_place) & (k_doc == q_doc)
                at = (level * len(theirs) + index) * half
                bias_refs[side][at : at + half, :] = jnp.where(allowed, 0.0, -1e30)


def attention_kernel(count, *refs):
    rank_ref, which_ref, lengths_ref, slots_ref, q_ref, g_ref, k_ref, v_ref = refs[:8]
    rest = refs[8:]
    received = rest[:count]
    out_ref, gq_ref, own_ref = rest[count : count + 3]
    back = rest[count + 3 : 2 * count + 3]
    bias_refs, valid_refs = rest[2 * count + 3 : 2 * count + 5], rest[2 * count + 5 : 2 * count + 7]
    kk, vv, kt_ref, vt_ref = rest[2 * count + 7 :]
    half = q_ref.shape[0] // 2
    heads = kk.shape[0]
    lows = (count + 1) * half
    rank = rank_ref[0]
    ranks = [rank] + [rank ^ which_ref[index + 1] for index in range(count)]
    theirs = [block_places(slots_ref, other, half) for other in ranks]

    @pl.when(pl.program_id(0) == 0)
    def _():
        mask_scores(theirs, lengths_ref, bias_refs, valid_refs)

    for head in range(heads):
        cols = slice(head * HD, (head + 1) * HD)
        for level in range(2):
            for index, (_, rows) in enumerate(theirs):
                at = level * lows + index * half
                rows = rows[level]
                if index == 0:
                    kk[head, at : at + half] = k_ref[rows, cols]
                    vv[head, at : at + half] = v_ref[rows, cols]
                else:
                    kk[head, at : at + half] = received[index - 1][0, rows, cols]
                    vv[head, at : at + half] = received[index - 1][1, rows, cols]
        kt_ref[head] = kk[head].T
        vt_ref[head] = vv[head].T
    repeats = GROUP * half // valid_refs[0].shape[1]
    partial = {}

    def steps(head, side):
        size = (side + 1) * lows
        rows = theirs[0][1][side]
        key, value = kk[head, 0:size], vv[head, 0:size]
        columns = [slice(at * HD, (at + 1) * HD) for at in range(head * GROUP, (head + 1) * GROUP)]
        q = jnp.concatenate([q_ref[rows, cols] for cols in columns], axis=0)
        g_t = jnp.concatenate([g_ref[rows, cols] for cols in columns], axis=0).T
        scores = dot_nt(key, q)
        yield
        bias = jnp.concatenate([bias_refs[side][...]] * repeats, axis=1)
        valid = jnp.concatenate([valid_refs[side][...]] * repeats, axis=1)
        scores = scores * (FACTOR * LOG2E) + bias
        probs = jnp.exp2(scores - jnp.max(scores, axis=0, keepdims=True))
        inverse = 1.0 / jnp.sum(probs, axis=0, keepdims=True)
        probs_b = probs.astype(BF16)
        g_t = (g_t.astype(F32) * (inverse * valid)).astype(BF16)
        yield
        out_t = dot(vt_ref[head, :, 0:size], probs_b)
        dprob = dot(value, g_t)
        grad_v = dot_nt(probs_b, g_t)
        yield
        out_t = (out_t * inverse).astype(BF16)
        delta = jnp.sum(g_t.astype(F32) * out_t.astype(F32), axis=0, keepdims=True)
        dscore = (probs * (dprob - delta)).astype(BF16)
        yield
        gq_t = dot(kt_ref[head, :, 0:size], dscore)
        grad_k = dot(dscore, q)
        yield
        out = out_t.T
        gq = (gq_t * FACTOR).astype(BF16).T
        for index, cols in enumerate(columns):
            out_ref[rows, cols] = out[index * half : (index + 1) * half]
            gq_ref[rows, cols] = gq[index * half : (index + 1) * half]
        partial[head, side] = (grad_k * FACTOR, grad_v)

    waiting = [steps(head, side) for head in range(heads) for side in (1, 0)]
    running = []
    while waiting or running:
        if waiting:
            running.append(waiting.pop(0))
        running = [chain for chain in running if next(chain, running) is not running]

    for head in range(heads):
        cols = slice(head * HD, (head + 1) * HD)
        for which in range(2):
            high, low = partial[head, 1][which], partial[head, 0][which]
            for level in range(2):
                for index, (_, rows) in enumerate(theirs):
                    at = level * lows + index * half
                    piece = high[at : at + half]
                    if level == 0:
                        piece = piece + low[at : at + half]
                    if index == 0:
                        own_ref[which, rows[level], cols] = piece
                    else:
                        back[index - 1][which, rows[level], cols] = piece.astype(BF16)


def attention(rank, which, lengths, slots, queries, grad_out, keys, values, received):
    count = len(received)
    tok = queries.shape[1]
    kv_heads = keys.shape[2] // HD
    heads = 2
    wide = GROUP * HD * heads
    rows = (count + 1) * tok
    smem = pl.BlockSpec(memory_space=pltpu.SMEM)
    row = pl.BlockSpec((None, tok, wide), lambda j: (0, 0, j))
    own = pl.BlockSpec((None, tok, HD * heads), lambda j: (0, 0, j))
    pair = pl.BlockSpec((2, tok, HD * heads), lambda j: (0, 0, j))
    flops = 6 * 2 * rows * tok * HD * GROUP * kv_heads
    moved = 4 * queries.size * 2 + (2 * count + 1) * received[0].size * 2
    return pl.pallas_call(
        functools.partial(attention_kernel, count),
        grid=(kv_heads // heads,),
        in_specs=[smem] * 4 + [row, row, own, own] + [pair] * count,
        out_specs=[row, row, pair] + [pair] * count,
        out_shape=[
            jax.ShapeDtypeStruct(queries.shape, BF16),
            jax.ShapeDtypeStruct(queries.shape, BF16),
            jax.ShapeDtypeStruct((2, tok, kv_heads * HD), F32),
        ]
        + [jax.ShapeDtypeStruct((2, tok, kv_heads * HD), BF16)] * count,
        scratch_shapes=[
            pltpu.VMEM((rows // 2, tok), F32),
            pltpu.VMEM((rows, tok), F32),
            pltpu.VMEM((1, tok), F32),
            pltpu.VMEM((1, tok), F32),
            pltpu.VMEM((heads, rows, HD), BF16),
            pltpu.VMEM((heads, rows, HD), BF16),
            pltpu.VMEM((heads, HD, rows), BF16),
            pltpu.VMEM((heads, HD, rows), BF16),
        ],
        compiler_params=pltpu.CompilerParams(vmem_limit_bytes=60 * 2**20),
        cost_estimate=pl.CostEstimate(
            flops=flops, bytes_accessed=moved, transcendentals=rows * tok * GROUP * kv_heads
        ),
        name="attention",
    )(rank, which, lengths, slots, queries, grad_out, keys, values, *received)


def prepare_kernel(choices, partners_ref, k_ref, v_ref, both_ref, which_ref):
    used = partners_ref[0, 0]
    for index in range(1, partners_ref.shape[0]):
        used = used | partners_ref[index, 0]
    found = [jnp.int32(0)] * which_ref.shape[0]
    for index, bits in enumerate(choices):
        hit = used == sum(1 << bit for bit in bits)
        wanted = [index] + [1 << bit for bit in bits]
        found = [jnp.where(hit, new, old) for new, old in zip(wanted, found)]
    for index, value in enumerate(found):
        which_ref[index] = value
    both_ref[0] = k_ref[0]
    both_ref[1] = v_ref[0]


def prepare(choices, partners, keys, values):
    vmem = pl.BlockSpec(memory_space=pltpu.VMEM)
    smem = pl.BlockSpec(memory_space=pltpu.SMEM)
    return pl.pallas_call(
        functools.partial(prepare_kernel, choices),
        in_specs=[smem, vmem, vmem],
        out_specs=[vmem, smem],
        out_shape=[
            jax.ShapeDtypeStruct((2,) + keys.shape[1:], BF16),
            jax.ShapeDtypeStruct((1 + partners.shape[0],), jnp.int32),
        ],
        compiler_params=pltpu.CompilerParams(vmem_limit_bytes=60 * 2**20),
        name="prepare",
    )(partners, keys, values)


def loss_weight(all_tokens, padding_refs, width):
    last = padding_refs[0].shape[1] - 1
    padded = padding_refs[0][0, last] + padding_refs[1][0, last]
    return F32(all_tokens) / jnp.full((1, width), all_tokens - padded, jnp.int32).astype(F32)


def finish_kernel(all_tokens, count, half_ref, other_ref, gq_ref, own_ref, *rest):
    parts, outs, scratch = rest[:count], rest[count : count + 3], rest[count + 3 :]
    scaled, summed, sems = scratch
    width = scaled.shape[2]
    weight = loss_weight(all_tokens, (half_ref, other_ref), width)
    copies = []

    def send(source, target):
        copy = pltpu.make_async_copy(source, target, sems.at[len(copies)])
        copy.start()
        copies.append(copy)

    for part in range(scaled.shape[0]):
        cols = slice(part * width, (part + 1) * width)
        scaled[part] = (gq_ref[0, :, cols].astype(F32) * weight).astype(BF16)
        send(scaled.at[part], outs[0].at[0, :, cols])
    for which in range(2):
        value = own_ref[which]
        for part in parts:
            value = value + part[which].astype(F32)
        summed[which] = (value * weight[:, : value.shape[1]]).astype(BF16)
        send(summed.at[which], outs[which + 1].at[0])
    for copy in copies:
        copy.wait()


def finish(all_tokens, half, other, grad_q, own, parts):
    smem = pl.BlockSpec(memory_space=pltpu.SMEM)
    vmem = pl.BlockSpec(memory_space=pltpu.VMEM)
    hbm = pl.BlockSpec(memory_space=pltpu.HBM)
    pieces = 4
    keys = jax.ShapeDtypeStruct((1,) + own.shape[1:], BF16)
    return pl.pallas_call(
        functools.partial(finish_kernel, all_tokens, len(parts)),
        in_specs=[smem, smem] + [vmem] * (2 + len(parts)),
        out_specs=[hbm] * 3,
        out_shape=[jax.ShapeDtypeStruct(grad_q.shape, BF16), keys, keys],
        scratch_shapes=[
            pltpu.VMEM((pieces, grad_q.shape[1], grad_q.shape[2] // pieces), BF16),
            pltpu.VMEM(own.shape, BF16),
            pltpu.SemaphoreType.DMA((pieces + 2,)),
        ],
        compiler_params=pltpu.CompilerParams(vmem_limit_bytes=60 * 2**20),
        name="finish",
    )(half, other, grad_q, own, *parts)


def fetch(bits, step, both, lengths):
    received = [swapped(both, "ctx", 1 << bit) for bit in bits]
    return received, lengths + swapped(lengths, "dp", step)


def give_back(bits, steps, back, padding):
    far, *near = reversed(list(zip(bits, back)))
    returned = [swapped(far[1], "ctx", 1 << far[0])]
    other = swapped(padding, "dp", steps[0])
    returned += [swapped(part, "ctx", 1 << bit) for bit, part in near]
    padding = padding + other
    return returned, padding, swapped(padding, "dp", steps[1])


def on_device(queries, keys, values, grad_out, doc_lengths, block_of_slot, partners):
    rounds = partners.shape[0]
    seqs, ranks = lax.axis_size("dp"), lax.axis_size("ctx")
    choices = list(itertools.combinations(range(ranks.bit_length() - 1), rounds))
    steps = [1 << step for step in reversed(range(seqs.bit_length() - 1))]
    rank = lax.axis_index("ctx").astype(jnp.int32).reshape(1)
    both, which = prepare(choices, partners, keys, values)
    fetches = [functools.partial(fetch, bits, steps[0]) for bits in choices]
    received, padding = lax.switch(which[0], fetches, both, doc_lengths)
    other = swapped(padding, "dp", steps[1])
    attended, grad_q, own, *back = attention(
        rank, which, doc_lengths, block_of_slot, queries, grad_out, keys, values, received
    )
    other, back = lax.optimization_barrier((other, back))
    gives = [functools.partial(give_back, bits, steps[2:]) for bits in choices]
    returned, padding, other = lax.switch(which[0], gives, back, padding + other)
    all_tokens = seqs * ranks * queries.shape[1]
    grad_q, grad_k, grad_v = finish(all_tokens, padding, other, grad_q, own, returned)
    return attended, grad_q, grad_k, grad_v


def solution(mesh):
    rows = P("dp", "ctx", None)
    in_specs = (rows, rows, rows, rows, P("dp", None), P(), P())
    return jax.shard_map(
        on_device, mesh=mesh, in_specs=in_specs, out_specs=(rows,) * 4, check_vma=False
    )
```

profile of v0, /device:TPU:8, one launch (start us, length us, event | category | flops | bytes accessed | tf_op | source)
XLA Modules:
  0.0 71.6 jit_solution(6777514584070171236)
XLA Ops:
  0.6 1.5 %prepare.1 = (bf16[2,128,512]{2,1,0:T(8,128)(2,1)S(1)}, s32[4]{0:T(128)}) custom-call(s32[3,32]{1,0:T(4,128)} %partners_ref.1, bf16[1,128,512]{2,1,0:T(8,128)(2,1)} %refs_6_.1, bf16[1,128,512]{2,1,0:T(8,128)(2,1)} %refs_7_.1), custom_call_target="tpu_custom_call" | custom-call | tf_op jit(solution)/shard_map/prepare/pallas_call | solution.py:224
  2.2 0.0 copy-start
  2.2 0.6 copy-done
  2.8 0.0 copy-start.1
  2.9 0.6 copy-done.1
  3.5 22.0 %conditional.2 = (bf16[2,128,512]{2,1,0:T(8,128)(2,1)}, bf16[2,128,512]{2,1,0:T(8,128)(2,1)}, bf16[2,128,512]{2,1,0:T(8,128)(2,1)}, s32[1,8]{1,0:T(1,128)S(1)}, s32[1,8]{1,0:T(1,128)S(1)}, /*index=5*/s32[1,8]{1,0:T(1,128)}) conditional(s32[]{:T(128)} %bitcast.1, (bf16[2,128,512]{2,1,0:T(8,128)(2,1)S(1)}, ...), branch_computations={%region_0.0_spmd, %region_1.0_spmd, %region_2.0_spmd, %region_3.0_... | conditional | bytes 3146064 | solution.py:312
  3.5 4.5 %collective-permute-start.38 = (bf16[2,128,512]{2,1,0:T(8,128)(2,1)S(1)}, bf16[2,128,512]{2,1,0:T(8,128)(2,1)}, u32[]{:S(2)}, u32[]{:S(2)}) collective-permute-start(bf16[2,128,512]{2,1,0:T(8,128)(2,1)S(1)} %get-tuple-element.144), channel_id=1, source_target_pairs={{0,16},{1,17},{2,18},{3,19},{4,20},{5,21},{6,22},{7,23},{8,24},{9,... | collective-permute-start | bytes 786440 | tf_op jit(solution)/shard_map/cond/branch_9_fun/ppermute | solution.py:23
  8.0 5.2 %collective-permute-start.37 = (bf16[2,128,512]{2,1,0:T(8,128)(2,1)S(1)}, bf16[2,128,512]{2,1,0:T(8,128)(2,1)}, u32[]{:S(2)}, u32[]{:S(2)}) collective-permute-start(bf16[2,128,512]{2,1,0:T(8,128)(2,1)S(1)} %get-tuple-element.144), channel_id=1, source_target_pairs={{0,8},{1,9},{2,10},{3,11},{4,12},{5,13},{6,14},{7,15},{8,0},{9,1},... | collective-permute-start | bytes 786440 | tf_op jit(solution)/shard_map/cond/branch_9_fun/ppermute | solution.py:23
  13.1 2.1 %collective-permute-start.36 = (bf16[2,128,512]{2,1,0:T(8,128)(2,1)S(1)}, bf16[2,128,512]{2,1,0:T(8,128)(2,1)}, u32[]{:S(2)}, u32[]{:S(2)}) collective-permute-start(bf16[2,128,512]{2,1,0:T(8,128)(2,1)S(1)} %get-tuple-element.144), channel_id=1, source_target_pairs={{0,4},{1,5},{2,6},{3,7},{4,0},{5,1},{6,2},{7,3},{8,12},{9,13},{10,... | collective-permute-start | bytes 786440 | tf_op jit(solution)/shard_map/cond/branch_9_fun/ppermute | solution.py:23
  15.3 5.9 %collective-permute-start.39 = (s32[1,8]{1,0:T(1,128)S(1)}, s32[1,8]{1,0:T(1,128)}, u32[]{:S(2)}, u32[]{:S(2)}) collective-permute-start(s32[1,8]{1,0:T(1,128)S(1)} %get-tuple-element.298), channel_id=1, source_target_pairs={{0,256},{32,288},{64,320},{96,352},{128,384},{160,416},{192,448},{... | collective-permute-start | bytes 104 | tf_op jit(solution)/shard_map/cond/branch_9_fun/ppermute | solution.py:23
  21.2 4.2 %collective-permute-done.39 = s32[1,8]{1,0:T(1,128)} collective-permute-done((s32[1,8]{1,0:T(1,128)S(1)}, s32[1,8]{1,0:T(1,128)}, u32[]{:S(2)}, u32[]{:S(2)}) %collective-permute-start.39) | collective-permute-done | bytes 64 | tf_op jit(solution)/shard_map/cond/branch_9_fun/ppermute | solution.py:23
  25.4 0.0 collective-permute-done.38
  25.4 0.0 collective-permute-done.37
  25.4 0.0 collective-permute-done.36
  25.4 0.6 add.46
  26.1 10.9 %collective-permute-start.90 = (s32[1,8]{1,0:T(1,128)S(1)}, s32[1,8]{1,0:T(1,128)S(1)}, u32[]{:S(2)}, u32[]{:S(2)}) collective-permute-start(s32[1,8]{1,0:T(1,128)S(1)} %add.46), channel_id=1, source_target_pairs={{0,128},{32,160},{64,192},{96,224},{128,0},{160,32},{192,64},{224,... | collective-permute-start | bytes 104 | tf_op jit(solution)/shard_map/ppermute | solution.py:23
  37.0 8.4 %attention.1 = (bf16[1,128,4096]{2,1,0:T(8,128)(2,1)}, bf16[1,128,4096]{2,1,0:T(8,128)(2,1)}, f32[2,128,512]{2,1,0:T(8,128)}, bf16[2,128,512]{2,1,0:T(8,128)(2,1...) custom-call(s32[1]{0:T(128)} %bitcast.refs_0_, s32[4]{0:T(128)} %get-tuple-element.215.refs_1_, ...), custom_call_target="tpu_custom_call" | custom-call | flops 3221225472 | bytes 6029312 | tf_op jit(solution)/shard_map/attention/pallas_call | solution.py:177
  45.4 0.0 collective-permute-done.90
  45.4 23.5 %conditional.3 = (bf16[2,128,512]{2,1,0:T(8,128)(2,1)}, bf16[2,128,512]{2,1,0:T(8,128)(2,1)}, bf16[2,128,512]{2,1,0:T(8,128)(2,1)}, s32[1,8]{1,0:T(1,128)}, s32[1,8]{1,0:T(1,128)}) conditional(s32[]{:T(128)} %bitcast.1, (bf16[2,128,512]{2,1,0:T(8,128)(2,1)S(1)}, bf16[2,128,512]{2,1,0:T(8,128)(2,1)S(1)}, ...), branch_computations={%region_10.0_spmd, %region_11.0_spmd, %region_12.0_spmd, %region_1... | conditional | flops 8 | bytes 3146320 | solution.py:319
  45.4 1.9 %collective-permute-start.85 = (bf16[2,128,512]{2,1,0:T(8,128)(2,1)S(1)}, bf16[2,128,512]{2,1,0:T(8,128)(2,1)}, u32[]{:S(2)}, u32[]{:S(2)}) collective-permute-start(bf16[2,128,512]{2,1,0:T(8,128)(2,1)S(1)} %get-tuple-element.182), channel_id=1, source_target_pairs={{0,16},{1,17},{2,18},{3,19},{4,20},{5,21},{6,22},{7,23},{8,24},{9,... | collective-permute-start | bytes 786440 | tf_op jit(solution)/shard_map/cond/branch_9_fun/ppermute | solution.py:23
  47.4 4.0 %collective-permute-start.86 = (bf16[2,128,512]{2,1,0:T(8,128)(2,1)S(1)}, bf16[2,128,512]{2,1,0:T(8,128)(2,1)}, u32[]{:S(2)}, u32[]{:S(2)}) collective-permute-start(bf16[2,128,512]{2,1,0:T(8,128)(2,1)S(1)} %get-tuple-element.183), channel_id=1, source_target_pairs={{0,8},{1,9},{2,10},{3,11},{4,12},{5,13},{6,14},{7,15},{8,0},{9,1},... | collective-permute-start | bytes 786440 | tf_op jit(solution)/shard_map/cond/branch_9_fun/ppermute | solution.py:23
  51.4 4.9 %collective-permute-start.87 = (bf16[2,128,512]{2,1,0:T(8,128)(2,1)S(1)}, bf16[2,128,512]{2,1,0:T(8,128)(2,1)}, u32[]{:S(2)}, u32[]{:S(2)}) collective-permute-start(bf16[2,128,512]{2,1,0:T(8,128)(2,1)S(1)} %get-tuple-element.184), channel_id=1, source_target_pairs={{0,4},{1,5},{2,6},{3,7},{4,0},{5,1},{6,2},{7,3},{8,12},{9,13},{10,... | collective-permute-start | bytes 786440 | tf_op jit(solution)/shard_map/cond/branch_9_fun/ppermute | solution.py:23
  56.3 4.3 %collective-permute-start.88 = (s32[1,8]{1,0:T(1,128)S(1)}, s32[1,8]{1,0:T(1,128)S(1)}, u32[]{:S(2)}, u32[]{:S(2)}) collective-permute-start(s32[1,8]{1,0:T(1,128)S(1)} %get-tuple-element.185), channel_id=1, source_target_pairs={{0,64},{32,96},{64,0},{96,32},{128,192},{160,224},{192,128},{224,1... | collective-permute-start | bytes 104 | tf_op jit(solution)/shard_map/cond/branch_9_fun/ppermute | solution.py:23
  60.6 2.0 %collective-permute-done.88 = s32[1,8]{1,0:T(1,128)S(1)} collective-permute-done((s32[1,8]{1,0:T(1,128)S(1)}, s32[1,8]{1,0:T(1,128)S(1)}, u32[]{:S(2)}, u32[]{:S(2)}) %collective-permute-start.88) | collective-permute-done | bytes 64 | tf_op jit(solution)/shard_map/cond/branch_9_fun/ppermute | solution.py:23
  62.7 0.6 add.43
  63.3 3.4 %collective-permute-start.89 = (s32[1,8]{1,0:T(1,128)}, s32[1,8]{1,0:T(1,128)}, u32[]{:S(2)}, u32[]{:S(2)}) collective-permute-start(s32[1,8]{1,0:T(1,128)} %add.43), channel_id=1, source_target_pairs={{0,32},{32,0},{64,96},{96,64},{128,160},{160,128},{192,224},{224,1... | collective-permute-start | bytes 104 | tf_op jit(solution)/shard_map/cond/branch_9_fun/ppermute | solution.py:23
  66.7 2.2 %collective-permute-done.89 = s32[1,8]{1,0:T(1,128)} collective-permute-done((s32[1,8]{1,0:T(1,128)}, s32[1,8]{1,0:T(1,128)}, u32[]{:S(2)}, u32[]{:S(2)}) %collective-permute-start.89) | collective-permute-done | bytes 64 | tf_op jit(solution)/shard_map/cond/branch_9_fun/ppermute | solution.py:23
  68.9 0.0 collective-permute-done.85
  68.9 0.0 collective-permute-done.86
  68.9 0.0 collective-permute-done.87
  68.9 2.7 %finish.1 = (bf16[1,128,4096]{2,1,0:T(8,128)(2,1)}, bf16[1,128,512]{2,1,0:T(8,128)(2,1)}, bf16[1,128,512]{2,1,0:T(8,128)(2,1)}) custom-call(s32[1,8]{1,0:T(1,128)} %get-tuple-element.230.half_ref, s32[1,8]{1,0:T(1,128)} %get-tuple-element.231.other_ref, bf16[1,128,4096]{2,1,0:T(8,128)(2,1)} %get-tuple-element.232.gq_ref, ...), custom_call_target="tpu_custom_call" | custom-call | tf_op jit(solution)/shard_map/finish/pallas_call | solution.py:275
  (1 shorter events, 0.0 us)
Async XLA Ops:
  2.2 0.7 copy-start
  2.8 0.7 copy-start.1
  3.5 22.0 %collective-permute-start.38 = (bf16[2,128,512]{2,1,0:T(8,128)(2,1)S(1)}, bf16[2,128,512]{2,1,0:T(8,128)(2,1)}, u32[]{:S(2)}, u32[]{:S(2)}) collective-permute-start(bf16[2,128,512]{2,1,0:T(8,128)(2,1)S(1)} %get-tuple-element.144), channel_id=1, source_target_pairs={{0,16},{1,17},{2,18},{3,19},{4,20},{5,21},{6,22},{7,23},{8,24},{9,... | collective-permute-start | bytes 786440 | tf_op jit(solution)/shard_map/cond/branch_9_fun/ppermute | solution.py:23
  8.0 17.5 %collective-permute-start.37 = (bf16[2,128,512]{2,1,0:T(8,128)(2,1)S(1)}, bf16[2,128,512]{2,1,0:T(8,128)(2,1)}, u32[]{:S(2)}, u32[]{:S(2)}) collective-permute-start(bf16[2,128,512]{2,1,0:T(8,128)(2,1)S(1)} %get-tuple-element.144), channel_id=1, source_target_pairs={{0,8},{1,9},{2,10},{3,11},{4,12},{5,13},{6,14},{7,15},{8,0},{9,1},... | collective-permute-start | bytes 786440 | tf_op jit(solution)/shard_map/cond/branch_9_fun/ppermute | solution.py:23
  13.1 12.3 %collective-permute-start.36 = (bf16[2,128,512]{2,1,0:T(8,128)(2,1)S(1)}, bf16[2,128,512]{2,1,0:T(8,128)(2,1)}, u32[]{:S(2)}, u32[]{:S(2)}) collective-permute-start(bf16[2,128,512]{2,1,0:T(8,128)(2,1)S(1)} %get-tuple-element.144), channel_id=1, source_target_pairs={{0,4},{1,5},{2,6},{3,7},{4,0},{5,1},{6,2},{7,3},{8,12},{9,13},{10,... | collective-permute-start | bytes 786440 | tf_op jit(solution)/shard_map/cond/branch_9_fun/ppermute | solution.py:23
  15.3 10.1 %collective-permute-start.39 = (s32[1,8]{1,0:T(1,128)S(1)}, s32[1,8]{1,0:T(1,128)}, u32[]{:S(2)}, u32[]{:S(2)}) collective-permute-start(s32[1,8]{1,0:T(1,128)S(1)} %get-tuple-element.298), channel_id=1, source_target_pairs={{0,256},{32,288},{64,320},{96,352},{128,384},{160,416},{192,448},{... | collective-permute-start | bytes 104 | tf_op jit(solution)/shard_map/cond/branch_9_fun/ppermute | solution.py:23
  26.1 19.3 %collective-permute-start.90 = (s32[1,8]{1,0:T(1,128)S(1)}, s32[1,8]{1,0:T(1,128)S(1)}, u32[]{:S(2)}, u32[]{:S(2)}) collective-permute-start(s32[1,8]{1,0:T(1,128)S(1)} %add.46), channel_id=1, source_target_pairs={{0,128},{32,160},{64,192},{96,224},{128,0},{160,32},{192,64},{224,... | collective-permute-start | bytes 104 | tf_op jit(solution)/shard_map/ppermute | solution.py:23
  45.4 23.4 %collective-permute-start.85 = (bf16[2,128,512]{2,1,0:T(8,128)(2,1)S(1)}, bf16[2,128,512]{2,1,0:T(8,128)(2,1)}, u32[]{:S(2)}, u32[]{:S(2)}) collective-permute-start(bf16[2,128,512]{2,1,0:T(8,128)(2,1)S(1)} %get-tuple-element.182), channel_id=1, source_target_pairs={{0,16},{1,17},{2,18},{3,19},{4,20},{5,21},{6,22},{7,23},{8,24},{9,... | collective-permute-start | bytes 786440 | tf_op jit(solution)/shard_map/cond/branch_9_fun/ppermute | solution.py:23
  47.4 21.5 %collective-permute-start.86 = (bf16[2,128,512]{2,1,0:T(8,128)(2,1)S(1)}, bf16[2,128,512]{2,1,0:T(8,128)(2,1)}, u32[]{:S(2)}, u32[]{:S(2)}) collective-permute-start(bf16[2,128,512]{2,1,0:T(8,128)(2,1)S(1)} %get-tuple-element.183), channel_id=1, source_target_pairs={{0,8},{1,9},{2,10},{3,11},{4,12},{5,13},{6,14},{7,15},{8,0},{9,1},... | collective-permute-start | bytes 786440 | tf_op jit(solution)/shard_map/cond/branch_9_fun/ppermute | solution.py:23
  51.4 17.5 %collective-permute-start.87 = (bf16[2,128,512]{2,1,0:T(8,128)(2,1)S(1)}, bf16[2,128,512]{2,1,0:T(8,128)(2,1)}, u32[]{:S(2)}, u32[]{:S(2)}) collective-permute-start(bf16[2,128,512]{2,1,0:T(8,128)(2,1)S(1)} %get-tuple-element.184), channel_id=1, source_target_pairs={{0,4},{1,5},{2,6},{3,7},{4,0},{5,1},{6,2},{7,3},{8,12},{9,13},{10,... | collective-permute-start | bytes 786440 | tf_op jit(solution)/shard_map/cond/branch_9_fun/ppermute | solution.py:23
  56.3 6.3 %collective-permute-start.88 = (s32[1,8]{1,0:T(1,128)S(1)}, s32[1,8]{1,0:T(1,128)S(1)}, u32[]{:S(2)}, u32[]{:S(2)}) collective-permute-start(s32[1,8]{1,0:T(1,128)S(1)} %get-tuple-element.185), channel_id=1, source_target_pairs={{0,64},{32,96},{64,0},{96,32},{128,192},{160,224},{192,128},{224,1... | collective-permute-start | bytes 104 | tf_op jit(solution)/shard_map/cond/branch_9_fun/ppermute | solution.py:23
  63.3 5.6 %collective-permute-start.89 = (s32[1,8]{1,0:T(1,128)}, s32[1,8]{1,0:T(1,128)}, u32[]{:S(2)}, u32[]{:S(2)}) collective-permute-start(s32[1,8]{1,0:T(1,128)} %add.43), channel_id=1, source_target_pairs={{0,32},{32,0},{64,96},{96,64},{128,160},{160,128},{192,224},{224,1... | collective-permute-start | bytes 104 | tf_op jit(solution)/shard_map/cond/branch_9_fun/ppermute | solution.py:23
where the time goes:
time: 71.3 us; the launch traced here: 71.6 us
  starting transfers between devices  47.2 us (66%)
  Pallas kernels  12.6 us (18%)
  waiting for transfers between devices  8.46 us (12%)
  local copies, waits for them, and re-layouts  1.26 us (2%)
  other arithmetic  1.24 us (2%)
  between operations  0.72 us (1%)
    ppermute x10, starting transfers between devices, swapped(): return lax.ppermute(value, axis, pairs)  47.2 us
    ppermute x10, waiting for transfers between devices, swapped(): return lax.ppermute(value, axis, pairs)  8.46 us
    pallas_call x1, Pallas kernels, attention(): pl.pallas_call(functools.partial(attention_kernel, count), grid=(kv_heads...  8.36 us
    pallas_call x1, Pallas kernels, finish(): pl.pallas_call(functools.partial(finish_kernel, all_tokens, len(parts)),...  2.74 us
    pallas_call x1, Pallas kernels, prepare(): pl.pallas_call(functools.partial(prepare_kernel, choices), in_specs=[smem...  1.52 us
  transfers between devices with their start and end apart: 10, of which 3 were waited for; matrix products, arithmetic and copies ran while one was open for 1% of the time, Pallas kernels for 12%

commit v1 on v0

--- a/solution.py
+++ b/solution.py
@@ -236,55 +236,39 @@
 
 def loss_weight(all_tokens, padding_refs, width):
     last = padding_refs[0].shape[1] - 1
-    padded = padding_refs[0][0, last] + padding_refs[1][0, last]
+    padded = sum([ref[0, last] for ref in padding_refs])
     return F32(all_tokens) / jnp.full((1, width), all_tokens - padded, jnp.int32).astype(F32)
 
 
-def finish_kernel(all_tokens, count, half_ref, other_ref, gq_ref, own_ref, *rest):
-    parts, outs, scratch = rest[:count], rest[count : count + 3], rest[count + 3 :]
-    scaled, summed, sems = scratch
-    width = scaled.shape[2]
-    weight = loss_weight(all_tokens, (half_ref, other_ref), width)
-    copies = []
-
-    def send(source, target):
-        copy = pltpu.make_async_copy(source, target, sems.at[len(copies)])
-        copy.start()
-        copies.append(copy)
-
-    for part in range(scaled.shape[0]):
-        cols = slice(part * width, (part + 1) * width)
-        scaled[part] = (gq_ref[0, :, cols].astype(F32) * weight).astype(BF16)
-        send(scaled.at[part], outs[0].at[0, :, cols])
-    for which in range(2):
+def finish_kernel(all_tokens, counts, *refs):
+    padding_refs, (gq_ref, own_ref, *rest) = refs[:counts], refs[counts:]
+    *parts, scaled_ref, gk_ref, gv_ref = rest
+    weight = loss_weight(all_tokens, padding_refs, gq_ref.shape[2])
+    scaled_ref[0] = (gq_ref[0].astype(F32) * weight).astype(BF16)
+    for which, out_ref in enumerate((gk_ref, gv_ref)):
         value = own_ref[which]
         for part in parts:
             value = value + part[which].astype(F32)
-        summed[which] = (value * weight[:, : value.shape[1]]).astype(BF16)
-        send(summed.at[which], outs[which + 1].at[0])
-    for copy in copies:
-        copy.wait()
-
-
-def finish(all_tokens, half, other, grad_q, own, parts):
+        out_ref[0] = (value * weight[:, : value.shape[1]]).astype(BF16)
+
+
+def finish(all_tokens, paddings, grad_q, own, parts):
+    steps = 4
+    rows = grad_q.shape[1]
     smem = pl.BlockSpec(memory_space=pltpu.SMEM)
-    vmem = pl.BlockSpec(memory_space=pltpu.VMEM)
-    hbm = pl.BlockSpec(memory_space=pltpu.HBM)
-    pieces = 4
+    wide = pl.BlockSpec((1, rows, grad_q.shape[2] // steps), lambda j: (0, 0, j))
+    pair = pl.BlockSpec((2, rows, own.shape[2] // steps), lambda j: (0, 0, j))
+    one = pl.BlockSpec((1, rows, own.shape[2] // steps), lambda j: (0, 0, j))
     keys = jax.ShapeDtypeStruct((1,) + own.shape[1:], BF16)
     return pl.pallas_call(
-        functools.partial(finish_kernel, all_tokens, len(parts)),
-        in_specs=[smem, smem] + [vmem] * (2 + len(parts)),
-        out_specs=[hbm] * 3,
+        functools.partial(finish_kernel, all_tokens, len(paddings)),
+        grid=(steps,),
+        in_specs=[smem] * len(paddings) + [wide, pair] + [pair] * len(parts),
+        out_specs=[wide, one, one],
         out_shape=[jax.ShapeDtypeStruct(grad_q.shape, BF16), keys, keys],
-        scratch_shapes=[
-            pltpu.VMEM((pieces, grad_q.shape[1], grad_q.shape[2] // pieces), BF16),
-            pltpu.VMEM(own.shape, BF16),
-            pltpu.SemaphoreType.DMA((pieces + 2,)),
-        ],
         compiler_params=pltpu.CompilerParams(vmem_limit_bytes=60 * 2**20),
         name="finish",
-    )(half, other, grad_q, own, *parts)
+    )(*paddings, grad_q, own, *parts)
 
 
 def fetch(bits, step, both, lengths):
@@ -293,12 +277,8 @@
 
 
 def give_back(bits, steps, back, padding):
-    far, *near = reversed(list(zip(bits, back)))
-    returned = [swapped(far[1], "ctx", 1 << far[0])]
-    other = swapped(padding, "dp", steps[0])
-    returned += [swapped(part, "ctx", 1 << bit) for bit, part in near]
-    padding = padding + other
-    return returned, padding, swapped(padding, "dp", steps[1])
+    returned = [swapped(part, "ctx", 1 << bit) for bit, part in list(zip(bits, back))[::-1]]
+    return returned, [swapped(padding, "dp", step) for step in steps]
 
 
 def on_device(queries, keys, values, grad_out, doc_lengths, block_of_slot, partners):
@@ -315,10 +295,11 @@
         rank, which, doc_lengths, block_of_slot, queries, grad_out, keys, values, received
     )
     other, back = lax.optimization_barrier((other, back))
-    gives = [functools.partial(give_back, bits, steps[2:]) for bits in choices]
-    returned, padding, other = lax.switch(which[0], gives, back, padding + other)
+    gives = [functools.partial(give_back, bits, (1, 2, 3)) for bits in choices]
+    padding = padding + other
+    returned, others = lax.switch(which[0], gives, back, padding)
     all_tokens = seqs * ranks * queries.shape[1]
-    grad_q, grad_k, grad_v = finish(all_tokens, padding, other, grad_q, own, returned)
+    grad_q, grad_k, grad_v = finish(all_tokens, [padding] + others, grad_q, own, returned)
     return attended, grad_q, grad_k, grad_v
 
 

time: 71.3 us -> 70.4 us (0.987)
  the two profiles are of different devices: /device:TPU:8 before, /device:TPU:1 now
where the time goes in v1:
time: 70.4 us; the launch traced here: 69.2 us
  starting transfers between devices  46.2 us (66%)
  Pallas kernels  13.6 us (19%)
  waiting for transfers between devices  6.66 us (9%)
  local copies, waits for them, and re-layouts  1.26 us (2%)
  between operations  0.73 us (1%)
    ppermute x11, starting transfers between devices, swapped(): return lax.ppermute(value, axis, pairs)  46.2 us
    pallas_call x1, Pallas kernels, attention(): pl.pallas_call(functools.partial(attention_kernel, count), grid=(kv_heads...  8.35 us
    ppermute x11, waiting for transfers between devices, swapped(): return lax.ppermute(value, axis, pairs)  6.66 us
    pallas_call x1, Pallas kernels, finish(): pl.pallas_call(functools.partial(finish_kernel, all_tokens, len(paddings)...  3.7 us
    pallas_call x1, Pallas kernels, prepare(): pl.pallas_call(functools.partial(prepare_kernel, choices), in_specs=[smem...  1.52 us
  transfers between devices with their start and end apart: 11, of which 3 were waited for; matrix products, arithmetic and copies ran while one was open for 0% of the time, Pallas kernels for 12%

profile of v1, /device:TPU:1, one launch (start us, length us, event | category | flops | bytes accessed | tf_op | source)
XLA Modules:
  0.0 69.2 jit_solution(13986385613529299323)
XLA Ops:
  0.6 1.5 %prepare.1 = (bf16[2,128,512]{2,1,0:T(8,128)(2,1)S(1)}, s32[4]{0:T(128)}) custom-call(s32[3,32]{1,0:T(4,128)} %partners_ref.1, bf16[1,128,512]{2,1,0:T(8,128)(2,1)} %refs_6_.1, bf16[1,128,512]{2,1,0:T(8,128)(2,1)} %refs_7_.1), custom_call_target="tpu_custom_call" | custom-call | tf_op jit(solution)/shard_map/prepare/pallas_call | solution.py:224
  2.2 0.0 copy-start
  2.2 0.6 copy-done
  2.8 0.0 copy-start.1
  2.9 0.6 copy-done.1
  3.5 21.0 %conditional.2 = (bf16[2,128,512]{2,1,0:T(8,128)(2,1)}, bf16[2,128,512]{2,1,0:T(8,128)(2,1)}, bf16[2,128,512]{2,1,0:T(8,128)(2,1)}, s32[1,8]{1,0:T(1,128)S(1)}, s32[1,8]{1,0:T(1,128)S(1)}, /*index=5*/s32[1,8]{1,0:T(1,128)}) conditional(s32[]{:T(128)} %bitcast.1, (bf16[2,128,512]{2,1,0:T(8,128)(2,1)S(1)}, ...), branch_computations={%region_0.0_spmd, %region_1.0_spmd, %region_2.0_spmd, %region_3.0_... | conditional | bytes 3146064 | solution.py:292
  3.5 5.0 %collective-permute-start.22 = (bf16[2,128,512]{2,1,0:T(8,128)(2,1)S(1)}, bf16[2,128,512]{2,1,0:T(8,128)(2,1)}, u32[]{:S(2)}, u32[]{:S(2)}) collective-permute-start(bf16[2,128,512]{2,1,0:T(8,128)(2,1)S(1)} %get-tuple-element.136), channel_id=1, source_target_pairs={{0,16},{1,17},{2,18},{3,19},{4,20},{5,21},{6,22},{7,23},{8,24},{9,... | collective-permute-start | bytes 786440 | tf_op jit(solution)/shard_map/cond/branch_5_fun/ppermute | solution.py:23
  8.5 3.2 %collective-permute-start.21 = (bf16[2,128,512]{2,1,0:T(8,128)(2,1)S(1)}, bf16[2,128,512]{2,1,0:T(8,128)(2,1)}, u32[]{:S(2)}, u32[]{:S(2)}) collective-permute-start(bf16[2,128,512]{2,1,0:T(8,128)(2,1)S(1)} %get-tuple-element.136), channel_id=1, source_target_pairs={{0,8},{1,9},{2,10},{3,11},{4,12},{5,13},{6,14},{7,15},{8,0},{9,1},... | collective-permute-start | bytes 786440 | tf_op jit(solution)/shard_map/cond/branch_5_fun/ppermute | solution.py:23
  11.7 4.4 %collective-permute-start.20 = (bf16[2,128,512]{2,1,0:T(8,128)(2,1)S(1)}, bf16[2,128,512]{2,1,0:T(8,128)(2,1)}, u32[]{:S(2)}, u32[]{:S(2)}) collective-permute-start(bf16[2,128,512]{2,1,0:T(8,128)(2,1)S(1)} %get-tuple-element.136), channel_id=1, source_target_pairs={{0,1},{1,0},{2,3},{3,2},{4,5},{5,4},{6,7},{7,6},{8,9},{9,8},{10,11... | collective-permute-start | bytes 786440 | tf_op jit(solution)/shard_map/cond/branch_5_fun/ppermute | solution.py:23
  16.1 3.5 %collective-permute-start.23 = (s32[1,8]{1,0:T(1,128)S(1)}, s32[1,8]{1,0:T(1,128)}, u32[]{:S(2)}, u32[]{:S(2)}) collective-permute-start(s32[1,8]{1,0:T(1,128)S(1)} %get-tuple-element.276), channel_id=1, source_target_pairs={{0,256},{32,288},{64,320},{96,352},{128,384},{160,416},{192,448},{... | collective-permute-start | bytes 104 | tf_op jit(solution)/shard_map/cond/branch_5_fun/ppermute | solution.py:23
  19.6 4.8 %collective-permute-done.23 = s32[1,8]{1,0:T(1,128)} collective-permute-done((s32[1,8]{1,0:T(1,128)S(1)}, s32[1,8]{1,0:T(1,128)}, u32[]{:S(2)}, u32[]{:S(2)}) %collective-permute-start.23) | collective-permute-done | bytes 64 | tf_op jit(solution)/shard_map/cond/branch_5_fun/ppermute | solution.py:23
  24.5 0.0 collective-permute-done.22
  24.5 0.0 collective-permute-done.21
  24.5 0.0 collective-permute-done.20
  24.5 0.7 add.10
  25.2 9.6 %collective-permute-start.100 = (s32[1,8]{1,0:T(1,128)S(1)}, s32[1,8]{1,0:T(1,128)S(1)}, u32[]{:S(2)}, u32[]{:S(2)}) collective-permute-start(s32[1,8]{1,0:T(1,128)S(1)} %add.10), channel_id=1, source_target_pairs={{0,128},{32,160},{64,192},{96,224},{128,0},{160,32},{192,64},{224,... | collective-permute-start | bytes 104 | tf_op jit(solution)/shard_map/ppermute | solution.py:23
  34.8 8.3 %attention.1 = (bf16[1,128,4096]{2,1,0:T(8,128)(2,1)}, bf16[1,128,4096]{2,1,0:T(8,128)(2,1)}, f32[2,128,512]{2,1,0:T(8,128)}, bf16[2,128,512]{2,1,0:T(8,128)(2,1...) custom-call(s32[1]{0:T(128)} %bitcast.refs_0_, s32[4]{0:T(128)} %get-tuple-element.216.refs_1_, ...), custom_call_target="tpu_custom_call" | custom-call | flops 3221225472 | bytes 6029312 | tf_op jit(solution)/shard_map/attention/pallas_call | solution.py:177
  43.2 0.0 collective-permute-done.100
  43.2 22.3 %conditional.3 = (bf16[2,128,512]{2,1,0:T(8,128)(2,1)}, bf16[2,128,512]{2,1,0:T(8,128)(2,1)}, bf16[2,128,512]{2,1,0:T(8,128)(2,1)}, s32[1,8]{1,0:T(1,128)}, s32[1,8]{1,0:T(1,128)}, /*index=5*/s32[1,8]{1,0:T(1,128)}) conditional(s32[]{:T(128)} %bitcast.1, (bf16[2,128,512]{2,1,0:T(8,128)(2,1)S(1)}, ...), branch_computations={%region_10.0_spmd, %region_11.0_spmd, %region_12.0_spmd, %region_1... | conditional | bytes 3146400 | solution.py:300
  43.2 4.7 %collective-permute-start.70 = (bf16[2,128,512]{2,1,0:T(8,128)(2,1)S(1)}, bf16[2,128,512]{2,1,0:T(8,128)(2,1)}, u32[]{:S(2)}, u32[]{:S(2)}) collective-permute-start(bf16[2,128,512]{2,1,0:T(8,128)(2,1)S(1)} %get-tuple-element.166), channel_id=1, source_target_pairs={{0,16},{1,17},{2,18},{3,19},{4,20},{5,21},{6,22},{7,23},{8,24},{9,... | collective-permute-start | bytes 786440 | tf_op jit(solution)/shard_map/cond/branch_5_fun/ppermute | solution.py:23
  48.0 2.1 %collective-permute-start.71 = (bf16[2,128,512]{2,1,0:T(8,128)(2,1)S(1)}, bf16[2,128,512]{2,1,0:T(8,128)(2,1)}, u32[]{:S(2)}, u32[]{:S(2)}) collective-permute-start(bf16[2,128,512]{2,1,0:T(8,128)(2,1)S(1)} %get-tuple-element.167), channel_id=1, source_target_pairs={{0,8},{1,9},{2,10},{3,11},{4,12},{5,13},{6,14},{7,15},{8,0},{9,1},... | collective-permute-start | bytes 786440 | tf_op jit(solution)/shard_map/cond/branch_5_fun/ppermute | solution.py:23
  50.1 4.3 %collective-permute-start.72 = (bf16[2,128,512]{2,1,0:T(8,128)(2,1)S(1)}, bf16[2,128,512]{2,1,0:T(8,128)(2,1)}, u32[]{:S(2)}, u32[]{:S(2)}) collective-permute-start(bf16[2,128,512]{2,1,0:T(8,128)(2,1)S(1)} %get-tuple-element.168), channel_id=1, source_target_pairs={{0,1},{1,0},{2,3},{3,2},{4,5},{5,4},{6,7},{7,6},{8,9},{9,8},{10,11... | collective-permute-start | bytes 786440 | tf_op jit(solution)/shard_map/cond/branch_5_fun/ppermute | solution.py:23
  54.4 4.9 %collective-permute-start.75 = (s32[1,8]{1,0:T(1,128)S(1)}, s32[1,8]{1,0:T(1,128)}, u32[]{:S(2)}, u32[]{:S(2)}) collective-permute-start(s32[1,8]{1,0:T(1,128)S(1)} %get-tuple-element.169), channel_id=1, source_target_pairs={{0,96},{32,64},{64,32},{96,0},{128,224},{160,192},{192,160},{224,1... | collective-permute-start | bytes 104 | tf_op jit(solution)/shard_map/cond/branch_5_fun/ppermute | solution.py:23
  59.3 1.9 %collective-permute-start.74 = (s32[1,8]{1,0:T(1,128)S(1)}, s32[1,8]{1,0:T(1,128)}, u32[]{:S(2)}, u32[]{:S(2)}) collective-permute-start(s32[1,8]{1,0:T(1,128)S(1)} %get-tuple-element.169), channel_id=1, source_target_pairs={{0,64},{32,96},{64,0},{96,32},{128,192},{160,224},{192,128},{224,1... | collective-permute-start | bytes 104 | tf_op jit(solution)/shard_map/cond/branch_5_fun/ppermute | solution.py:23
  61.2 0.0 collective-permute-done.75
  61.2 2.4 %collective-permute-start.73 = (s32[1,8]{1,0:T(1,128)S(1)}, s32[1,8]{1,0:T(1,128)}, u32[]{:S(2)}, u32[]{:S(2)}) collective-permute-start(s32[1,8]{1,0:T(1,128)S(1)} %get-tuple-element.169), channel_id=1, source_target_pairs={{0,32},{32,0},{64,96},{96,64},{128,160},{160,128},{192,224},{224,1... | collective-permute-start | bytes 104 | tf_op jit(solution)/shard_map/cond/branch_5_fun/ppermute | solution.py:23
  63.7 0.9 %collective-permute-done.74 = s32[1,8]{1,0:T(1,128)} collective-permute-done((s32[1,8]{1,0:T(1,128)S(1)}, s32[1,8]{1,0:T(1,128)}, u32[]{:S(2)}, u32[]{:S(2)}) %collective-permute-start.74) | collective-permute-done | bytes 64 | tf_op jit(solution)/shard_map/cond/branch_5_fun/ppermute | solution.py:23
  64.6 0.9 %collective-permute-done.73 = s32[1,8]{1,0:T(1,128)} collective-permute-done((s32[1,8]{1,0:T(1,128)S(1)}, s32[1,8]{1,0:T(1,128)}, u32[]{:S(2)}, u32[]{:S(2)}) %collective-permute-start.73) | collective-permute-done | bytes 64 | tf_op jit(solution)/shard_map/cond/branch_5_fun/ppermute | solution.py:23
  65.5 0.0 collective-permute-done.70
  65.5 0.0 collective-permute-done.71
  65.5 0.0 collective-permute-done.72
  65.5 3.7 %finish.1 = (bf16[1,128,4096]{2,1,0:T(8,128)(2,1)}, bf16[1,128,512]{2,1,0:T(8,128)(2,1)}, bf16[1,128,512]{2,1,0:T(8,128)(2,1)}) custom-call(s32[1,8]{1,0:T(1,128)S(1)} %add.12.refs_0_, s32[1,8]{1,0:T(1,128)} %get-tuple-element.231.refs_1_, s32[1,8]{1,0:T(1,128)} %get-tuple-element.232.refs_2_, s32[1,8]{1,0:T(1,128)} %get-tuple-element.233.refs_3_, ...), custom_call_target="tpu_custom_call" | custom-call | tf_op jit(solution)/shard_map/finish/pallas_call | solution.py:263
  (1 shorter events, 0.0 us)
Async XLA Ops:
  2.2 0.7 copy-start
  2.8 0.7 copy-start.1
  3.5 21.0 %collective-permute-start.22 = (bf16[2,128,512]{2,1,0:T(8,128)(2,1)S(1)}, bf16[2,128,512]{2,1,0:T(8,128)(2,1)}, u32[]{:S(2)}, u32[]{:S(2)}) collective-permute-start(bf16[2,128,512]{2,1,0:T(8,128)(2,1)S(1)} %get-tuple-element.136), channel_id=1, source_target_pairs={{0,16},{1,17},{2,18},{3,19},{4,20},{5,21},{6,22},{7,23},{8,24},{9,... | collective-permute-start | bytes 786440 | tf_op jit(solution)/shard_map/cond/branch_5_fun/ppermute | solution.py:23
  8.5 16.0 %collective-permute-start.21 = (bf16[2,128,512]{2,1,0:T(8,128)(2,1)S(1)}, bf16[2,128,512]{2,1,0:T(8,128)(2,1)}, u32[]{:S(2)}, u32[]{:S(2)}) collective-permute-start(bf16[2,128,512]{2,1,0:T(8,128)(2,1)S(1)} %get-tuple-element.136), channel_id=1, source_target_pairs={{0,8},{1,9},{2,10},{3,11},{4,12},{5,13},{6,14},{7,15},{8,0},{9,1},... | collective-permute-start | bytes 786440 | tf_op jit(solution)/shard_map/cond/branch_5_fun/ppermute | solution.py:23
  11.7 12.8 %collective-permute-start.20 = (bf16[2,128,512]{2,1,0:T(8,128)(2,1)S(1)}, bf16[2,128,512]{2,1,0:T(8,128)(2,1)}, u32[]{:S(2)}, u32[]{:S(2)}) collective-permute-start(bf16[2,128,512]{2,1,0:T(8,128)(2,1)S(1)} %get-tuple-element.136), channel_id=1, source_target_pairs={{0,1},{1,0},{2,3},{3,2},{4,5},{5,4},{6,7},{7,6},{8,9},{9,8},{10,11... | collective-permute-start | bytes 786440 | tf_op jit(solution)/shard_map/cond/branch_5_fun/ppermute | solution.py:23
  16.1 8.4 %collective-permute-start.23 = (s32[1,8]{1,0:T(1,128)S(1)}, s32[1,8]{1,0:T(1,128)}, u32[]{:S(2)}, u32[]{:S(2)}) collective-permute-start(s32[1,8]{1,0:T(1,128)S(1)} %get-tuple-element.276), channel_id=1, source_target_pairs={{0,256},{32,288},{64,320},{96,352},{128,384},{160,416},{192,448},{... | collective-permute-start | bytes 104 | tf_op jit(solution)/shard_map/cond/branch_5_fun/ppermute | solution.py:23
  25.2 18.0 %collective-permute-start.100 = (s32[1,8]{1,0:T(1,128)S(1)}, s32[1,8]{1,0:T(1,128)S(1)}, u32[]{:S(2)}, u32[]{:S(2)}) collective-permute-start(s32[1,8]{1,0:T(1,128)S(1)} %add.10), channel_id=1, source_target_pairs={{0,128},{32,160},{64,192},{96,224},{128,0},{160,32},{192,64},{224,... | collective-permute-start | bytes 104 | tf_op jit(solution)/shard_map/ppermute | solution.py:23
  43.2 22.3 %collective-permute-start.70 = (bf16[2,128,512]{2,1,0:T(8,128)(2,1)S(1)}, bf16[2,128,512]{2,1,0:T(8,128)(2,1)}, u32[]{:S(2)}, u32[]{:S(2)}) collective-permute-start(bf16[2,128,512]{2,1,0:T(8,128)(2,1)S(1)} %get-tuple-element.166), channel_id=1, source_target_pairs={{0,16},{1,17},{2,18},{3,19},{4,20},{5,21},{6,22},{7,23},{8,24},{9,... | collective-permute-start | bytes 786440 | tf_op jit(solution)/shard_map/cond/branch_5_fun/ppermute | solution.py:23
  48.0 17.5 %collective-permute-start.71 = (bf16[2,128,512]{2,1,0:T(8,128)(2,1)S(1)}, bf16[2,128,512]{2,1,0:T(8,128)(2,1)}, u32[]{:S(2)}, u32[]{:S(2)}) collective-permute-start(bf16[2,128,512]{2,1,0:T(8,128)(2,1)S(1)} %get-tuple-element.167), channel_id=1, source_target_pairs={{0,8},{1,9},{2,10},{3,11},{4,12},{5,13},{6,14},{7,15},{8,0},{9,1},... | collective-permute-start | bytes 786440 | tf_op jit(solution)/shard_map/cond/branch_5_fun/ppermute | solution.py:23
  50.1 15.4 %collective-permute-start.72 = (bf16[2,128,512]{2,1,0:T(8,128)(2,1)S(1)}, bf16[2,128,512]{2,1,0:T(8,128)(2,1)}, u32[]{:S(2)}, u32[]{:S(2)}) collective-permute-start(bf16[2,128,512]{2,1,0:T(8,128)(2,1)S(1)} %get-tuple-element.168), channel_id=1, source_target_pairs={{0,1},{1,0},{2,3},{3,2},{4,5},{5,4},{6,7},{7,6},{8,9},{9,8},{10,11... | collective-permute-start | bytes 786440 | tf_op jit(solution)/shard_map/cond/branch_5_fun/ppermute | solution.py:23
  54.4 6.9 %collective-permute-start.75 = (s32[1,8]{1,0:T(1,128)S(1)}, s32[1,8]{1,0:T(1,128)}, u32[]{:S(2)}, u32[]{:S(2)}) collective-permute-start(s32[1,8]{1,0:T(1,128)S(1)} %get-tuple-element.169), channel_id=1, source_target_pairs={{0,96},{32,64},{64,32},{96,0},{128,224},{160,192},{192,160},{224,1... | collective-permute-start | bytes 104 | tf_op jit(solution)/shard_map/cond/branch_5_fun/ppermute | solution.py:23
  59.3 5.3 %collective-permute-start.74 = (s32[1,8]{1,0:T(1,128)S(1)}, s32[1,8]{1,0:T(1,128)}, u32[]{:S(2)}, u32[]{:S(2)}) collective-permute-start(s32[1,8]{1,0:T(1,128)S(1)} %get-tuple-element.169), channel_id=1, source_target_pairs={{0,64},{32,96},{64,0},{96,32},{128,192},{160,224},{192,128},{224,1... | collective-permute-start | bytes 104 | tf_op jit(solution)/shard_map/cond/branch_5_fun/ppermute | solution.py:23
  61.2 4.2 %collective-permute-start.73 = (s32[1,8]{1,0:T(1,128)S(1)}, s32[1,8]{1,0:T(1,128)}, u32[]{:S(2)}, u32[]{:S(2)}) collective-permute-start(s32[1,8]{1,0:T(1,128)S(1)} %get-tuple-element.169), channel_id=1, source_target_pairs={{0,32},{32,0},{64,96},{96,64},{128,160},{160,128},{192,224},{224,1... | collective-permute-start | bytes 104 | tf_op jit(solution)/shard_map/cond/branch_5_fun/ppermute | solution.py:23
